TPU v7x, 512 devices: a whole 4x8x8 slice. The times are simulated.
512 devices in a mesh: row: 32 (over z_lo, y), col: 16 (over z_hi, x, core).
Axes of the slice: x: 4, y: 8, z: 8 (z_hi: 2, z_lo: 4; z = z_hi * 4 + z_lo), core: 2. Of those that a mesh axis runs over, the one named last changes fastest.
Arguments:
- center: bfloat16 [2048, 8192], P('col', 'row'), may hold values from -6 to 6
- radius: bfloat16 [2048, 8192], P('col', 'row'), may hold values from 0.049804688 to 1
- grad_center: bfloat16 [2048, 8192], P('row', 'col'), may hold values from -6 to 6
- grad_radius: bfloat16 [2048, 8192], P('row', 'col'), may hold values from -6 to 6
- weight: bfloat16 [8192, 8192], P('row', 'col'), may hold values from -0.0625 to 0.0625
- active: int32 [2048, 8192], P('col', 'row'), may hold values 0 or 1
Outputs:
- center_in: float32 [2048, 8192], P('col', 'row')
- radius_in: float32 [2048, 8192], P('col', 'row')
- weight_grad: float32 [8192, 8192], P('row', 'col')
All inputs are finite; a program needn't handle non-finite values. No bound on the sum of `active` on one device may be relied on, other than what follows from the above.
Results may differ from a plain program's by a relative error of at most 0.0003.
Values may be sent and summed in bfloat16 or wider, within the bound.
A program may use at most 64 MiB of HBM per device.

v0:
```python
import jax
import jax.numpy as jnp
from jax import lax
from jax.sharding import PartitionSpec as P


def on_device(center, radius, grad_center, grad_radius, weight, active):
    magnitude = jnp.abs(weight)
    stacked = jnp.stack((grad_center, grad_radius))
    inputs = lax.all_gather(jnp.stack((center, radius)), "col", axis=1, tiled=True)
    contract_out = (((1,), (1,)), ((), ()))
    contract_tok = (((0,), (0,)), ((), ()))
    total_tokens = inputs.shape[1]
    panels = lax.all_gather(stacked, "row", axis=1, tiled=True)
    through_center = lax.dot_general(
        panels[0], weight, contract_out, preferred_element_type=jnp.float32
    )
    through_radius = lax.dot_general(
        panels[1], magnitude, contract_out, preferred_element_type=jnp.float32
    )
    partial_terms = jnp.stack((through_center, through_radius))
    center_acc = lax.dot_general(
        inputs[0], panels[0], contract_tok, preferred_element_type=jnp.float32
    )
    radius_acc = lax.dot_general(
        inputs[1], panels[1], contract_tok, preferred_element_type=jnp.float32
    )
    center_acc, radius_acc = (center_acc, radius_acc)
    summed = lax.psum_scatter(partial_terms, "col", scatter_dimension=1, tiled=True)
    gating = active.astype(jnp.float32)
    center_in = gating * summed[0]
    radius_in = gating * summed[1]
    scale_factor = jnp.float32(1.0) / jnp.sqrt(jnp.float32(total_tokens))
    weight_grad = (center_acc + jnp.sign(weight).astype(jnp.float32) * radius_acc) * scale_factor
    return (center_in, radius_in, weight_grad)


def solution(mesh):
    in_specs = (
        P("col", "row"),
        P("col", "row"),
        P("row", "col"),
        P("row", "col"),
        P("row", "col"),
        P("col", "row"),
    )
    out_specs = (P("col", "row"), P("col", "row"), P("row", "col"))
    return jax.shard_map(
        on_device, mesh=mesh, in_specs=in_specs, out_specs=out_specs, check_vma=False
    )
```

profile of v0, /device:TPU:8, one launch (start us, length us, event | category | flops | bytes accessed | tf_op | source)
XLA Modules:
  0.0 365.3 jit_solution(8215343059179930053)
XLA Ops:
  7.2 0.0 all-gather.3.cloned.1.call-start
  7.2 1.5 pad_maximum_fusion.1
  8.8 0.0 all-gather.3.cloned.1.call-update
  8.8 0.0 all-gather.5.cloned.1.call-start
  8.8 1.5 pad_maximum_fusion.2
  10.4 0.0 all-gather.5.cloned.1.call-update
  10.4 0.0 copy-start.1
  10.4 0.0 reduce-scatter.2.cloned.1.call-start
  10.5 163.6 %all-gather.3.cloned.1.call-done = bf16[2,2048,512]{2,1,0:T(8,128)(2,1)} async-done(((bf16[2,64,512]{2,1,0:T(8,128)(2,1)}), bf16[2,2048,512]{2,1,0:T(8,128)(2,1)}) %all-gather.3.cloned.1.call-update) | async-done | bytes 4194320 | tf_op jit(solution)/shard_map/all_gather | solution.py:14
  174.1 0.0 copy-start
  174.1 2.5 convolution_bitcast_fusion.1
  176.6 0.0 copy-done.1
  176.6 0.4 copy-done
  177.0 0.7 convolution_bitcast_fusion
  177.7 2.2 pad_maximum_fusion
  180.0 0.0 reduce-scatter.2.cloned.1.call-update
  180.0 62.9 %all-gather.5.cloned.1.call-done = bf16[2,2048,256]{2,1,0:T(8,128)(2,1)} async-done(((bf16[2,128,256]{2,1,0:T(8,128)(2,1)}), bf16[2,2048,256]{2,1,0:T(8,128)(2,1)}) %all-gather.5.cloned.1.call-update) | async-done | bytes 2097168 | tf_op jit(solution)/shard_map/all_gather | solution.py:10
  242.9 0.0 copy-start.3
  242.9 2.8 fusion
  245.7 0.0 copy-done.3
  245.7 0.0 copy-start.2
  245.7 3.2 fusion.4
  248.9 108.1 %reduce-scatter.2.cloned.1.call-done = f32[2,128,256]{2,1,0:T(8,128)} async-done(((f32[2,2048,256]{2,1,0:T(8,128)}), f32[2,128,256]{2,1,0:T(8,128)}) %reduce-scatter.2.cloned.1.call-update) | async-done | bytes 262160 | tf_op jit(solution)/shard_map/reduce_scatter | solution.py:29
  357.1 0.0 copy-done.2
  357.1 1.7 fusion.6
Async XLA Ops:
  7.2 166.9 %all-gather.3.cloned.1.call-start = ((), (), s32[]{:S(2)}) async-start(), calls=%async_computation.1 | async-start | bytes 4325376 | tf_op jit(solution)/shard_map/all_gather | solution.py:14
  8.8 234.1 %all-gather.5.cloned.1.call-start = ((), (), s32[]{:S(2)}) async-start(), calls=%async_computation.3 | async-start | bytes 2228224 | tf_op jit(solution)/shard_map/all_gather | solution.py:10
  10.4 166.2 %copy-start.1 = (bf16[256,512]{1,0:T(8,128)(2,1)S(1)}, bf16[256,512]{1,0:T(8,128)(2,1)}, u32[]{:S(2)}) copy-start(bf16[256,512]{1,0:T(8,128)(2,1)} %param.10) | copy-start | bytes 786436
  10.4 346.6 %reduce-scatter.2.cloned.1.call-start = ((), (), s32[]{:S(2)}) async-start(), calls=%async_computation.2 | async-start | bytes 4456448 | tf_op jit(solution)/shard_map/reduce_scatter | solution.py:29
  174.1 2.9 copy-start
  242.9 2.8 copy-start.3
  245.7 111.3 %copy-start.2 = (s32[128,256]{1,0:T(8,128)S(1)}, s32[128,256]{1,0:T(8,128)}, u32[]{:S(2)}) copy-start(s32[128,256]{1,0:T(8,128)} %param.11) | copy-start | bytes 393220
Sparse Core Ops, SparseCore 0:
  10.7 163.3 all-gather.2
  178.0 64.8 all-gather.4
  247.8 109.1 reduce-scatter.1
where the time goes:
time: 366 us; the launch traced here: 365 us
  waiting for transfers between devices  335 us (92%)
  between operations  13.8 us (4%)
  matrix products  9.2 us (3%)
  other arithmetic  7.01 us (2%)
    all_gather x1, waiting for transfers between devices, on_device(): panels = lax.all_gather(stacked, 'row', axis=1, tiled=True)  164 us
    reduce_scatter x1, waiting for transfers between devices, on_device(): lax.psum_scatter(partial_terms, 'col', scatter_dimension=1, tiled=True)  108 us
    all_gather x1, waiting for transfers between devices, on_device(): lax.all_gather(jnp.stack((center, radius)), 'col', axis=1, tiled=True)  62.9 us
  transfers between devices with their start and end apart: 3, of which 3 were waited for; matrix products, arithmetic and copies ran while one was open for 4% of the time, Pallas kernels for 0%

commit v1 on v0

--- a/solution.py
+++ b/solution.py
@@ -1,7 +1,23 @@
+import functools
 import jax
 import jax.numpy as jnp
 from jax import lax
 from jax.sharding import PartitionSpec as P
+
+
+def _process_series_all(array_in, group_axis):
+    return jnp.concatenate(
+        jax.lax.all_to_all(
+            jnp.stack(tuple((array_in for _ in range(jax.lax.psum(1, group_axis)))), 0),
+            group_axis,
+            0,
+            0,
+        ),
+        axis=1,
+    )
+
+
+_pack_modes = functools.partial(_process_series_all, group_axis="row")
 
 
 def on_device(center, radius, grad_center, grad_radius, weight, active):
@@ -11,7 +27,7 @@
     contract_out = (((1,), (1,)), ((), ()))
     contract_tok = (((0,), (0,)), ((), ()))
     total_tokens = inputs.shape[1]
-    panels = lax.all_gather(stacked, "row", axis=1, tiled=True)
+    panels = _pack_modes(stacked)
     through_center = lax.dot_general(
         panels[0], weight, contract_out, preferred_element_type=jnp.float32
     )

time: 366 us -> 285 us (0.78)
  waiting for transfers between devices: 335 us -> 241 us
  starting transfers between devices: 0.12 us -> 13.4 us
  local copies, waits for them, and re-layouts: 0.41 us -> 5.62 us
    all_gather x1 -> x0, waiting for transfers between devices: 164 us -> none  [on_device(): panels = lax.all_gather(stacked, 'row', axis=1, tiled=True)]
    all_to_all x0 -> x1, waiting for transfers between devices: none -> 101 us  [_process_series_all(): jax.lax.all_to_all(jnp.stack(tuple((array_in for _ in range(jax.lax.psum(...]
    all_gather x1, waiting for transfers between devices: 62.9 us -> 26.5 us  [on_device(): lax.all_gather(jnp.stack((center, radius)), 'col', axis=1, tiled=True)]
    all_to_all x0 -> x1, starting transfers between devices: none -> 13.3 us  [_process_series_all(): jax.lax.all_to_all(jnp.stack(tuple((array_in for _ in range(jax.lax.psum(...]
    reduce_scatter x1, waiting for transfers between devices: 108 us -> 113 us  [on_device(): lax.psum_scatter(partial_terms, 'col', scatter_dimension=1, tiled=True)]
where the time goes in v1:
time: 285 us
  waiting for transfers between devices  241 us (85%)
  between operations  14.1 us (5%)
  starting transfers between devices  13.4 us (5%)
  matrix products  5.83 us (2%)
  local copies, waits for them, and re-layouts  5.62 us (2%)
  other arithmetic  5.46 us (2%)
    reduce_scatter x1, waiting for transfers between devices, on_device(): lax.psum_scatter(partial_terms, 'col', scatter_dimension=1, tiled=True)  113 us
    all_to_all x1, waiting for transfers between devices, _process_series_all(): jax.lax.all_to_all(jnp.stack(tuple((array_in for _ in range(jax.lax.psum(...  101 us
    all_gather x1, waiting for transfers between devices, on_device(): lax.all_gather(jnp.stack((center, radius)), 'col', axis=1, tiled=True)  26.5 us
    all_to_all x1, starting transfers between devices, _process_series_all(): jax.lax.all_to_all(jnp.stack(tuple((array_in for _ in range(jax.lax.psum(...  13.3 us
  transfers between devices with their start and end apart: 3, of which 3 were waited for; matrix products, arithmetic and copies ran while one was open for 4% of the time, Pallas kernels for 0%

profile of v1, /device:TPU:8, one launch (start us, length us, event | category | flops | bytes accessed | tf_op | source)
XLA Modules:
  0.0 285.0 jit_solution(14643400405816463906)
XLA Ops:
  7.2 0.9 pad_maximum_fusion.1
  8.1 2.5 stack.23
  10.5 0.0 copy-start.3
  10.5 0.0 copy-start.4
  10.5 13.3 %all-to-all-start = ((bf16[32,2,64,512]{3,2,1,0:T(8,128)(2,1)}), bf16[32,2,64,512]{3,2,1,0:T(8,128)(2,1)}, u32[]{:S(2)}, u32[]{:S(2)}) async-start(bf16[32,2,64,512]{3,2,1,0:T(8,128)(2,1)} %stack.23), calls=%async_computation | async-start | bytes 8388608 | tf_op jit(solution)/shard_map/all_to_all | solution.py:10
  23.9 0.0 all-gather.2.cloned.1.call-start
  23.9 0.0 copy-done.3
  23.9 0.0 copy-done.4
  23.9 0.7 pad_maximum_fusion.2
  24.6 0.0 all-gather.2.cloned.1.call-update
  24.6 0.0 reduce-scatter.2.cloned.1.call-start
  24.7 100.6 %all-to-all-done = bf16[32,2,64,512]{3,2,1,0:T(8,128)(2,1)} async-done(((bf16[32,2,64,512]{3,2,1,0:T(8,128)(2,1)}), bf16[32,2,64,512]{3,2,1,0:T(8,128)(2,1)}, u32[]{:S(2)}, u32[]{:S(2)}) %all-to-all-start) | async-done | bytes 4194336 | tf_op jit(solution)/shard_map/all_to_all | solution.py:10
  125.3 0.0 copy-start.1
  125.3 2.6 fusion.6
  127.9 0.0 copy-start
  127.9 0.0 copy-done.1
  127.9 0.7 convolution_bitcast_fusion.1
  128.6 0.6 copy-done
  129.2 0.7 convolution_bitcast_fusion
  129.9 2.2 pad_maximum_fusion
  132.2 0.0 reduce-scatter.2.cloned.1.call-update
  132.2 26.5 %all-gather.2.cloned.1.call-done = bf16[2,2048,256]{2,1,0:T(8,128)(2,1)} async-done(((bf16[2,128,256]{2,1,0:T(8,128)(2,1)}), bf16[2,2048,256]{2,1,0:T(8,128)(2,1)}) %all-gather.2.cloned.1.call-update) | async-done | bytes 2097168 | tf_op jit(solution)/shard_map/all_gather | solution.py:26
  158.6 0.0 copy-start.5
  158.6 2.8 fusion.2
  161.4 0.0 copy-done.5
  161.4 0.0 copy-start.2
  161.5 1.6 fusion.1
  163.0 113.4 %reduce-scatter.2.cloned.1.call-done = f32[2,128,256]{2,1,0:T(8,128)} async-done(((f32[2,2048,256]{2,1,0:T(8,128)}), f32[2,128,256]{2,1,0:T(8,128)}) %reduce-scatter.2.cloned.1.call-update) | async-done | bytes 262160 | tf_op jit(solution)/shard_map/reduce_scatter | solution.py:45
  276.4 0.0 copy-done.2
  276.4 1.7 fusion.4
Async XLA Ops:
  10.5 13.4 %copy-start.3 = (bf16[128,256]{1,0:T(8,128)(2,1)S(1)}, bf16[128,256]{1,0:T(8,128)(2,1)}, u32[]{:S(2)}) copy-start(bf16[128,256]{1,0:T(8,128)(2,1)} %param.7) | copy-start | bytes 196612
  10.5 13.4 %copy-start.4 = (bf16[128,256]{1,0:T(8,128)(2,1)S(1)}, bf16[128,256]{1,0:T(8,128)(2,1)}, u32[]{:S(2)}) copy-start(bf16[128,256]{1,0:T(8,128)(2,1)} %param.6) | copy-start | bytes 196612
  10.5 114.8 %all-to-all-start = ((bf16[32,2,64,512]{3,2,1,0:T(8,128)(2,1)}), bf16[32,2,64,512]{3,2,1,0:T(8,128)(2,1)}, u32[]{:S(2)}, u32[]{:S(2)}) async-start(bf16[32,2,64,512]{3,2,1,0:T(8,128)(2,1)} %stack.23), calls=%async_computation | async-start | bytes 8388608 | tf_op jit(solution)/shard_map/all_to_all | solution.py:10
  23.9 134.8 %all-gather.2.cloned.1.call-start = ((), (), s32[]{:S(2)}) async-start(), calls=%async_computation.3 | async-start | bytes 2228224 | tf_op jit(solution)/shard_map/all_gather | solution.py:26
  24.6 251.8 %reduce-scatter.2.cloned.1.call-start = ((), (), s32[]{:S(2)}) async-start(), calls=%async_computation.2 | async-start | bytes 4456448 | tf_op jit(solution)/shard_map/reduce_scatter | solution.py:45
  125.3 2.6 copy-start.1
  127.9 1.3 copy-start
  158.6 2.8 copy-start.5
  161.4 115.0 %copy-start.2 = (s32[128,256]{1,0:T(8,128)S(1)}, s32[128,256]{1,0:T(8,128)}, u32[]{:S(2)}) copy-start(s32[128,256]{1,0:T(8,128)} %param.11) | copy-start | bytes 393220
Sparse Core Ops, SparseCore 0:
  28.6 129.9 all-gather.1
  163.6 112.8 reduce-scatter.1
